TPU v7x, 32 devices: a whole 2x2x4 slice. The times are simulated.
32 devices in a mesh: group: 16 (over z, y, x), head: 2 (over core).
Axes of the slice: x: 2, y: 2, z: 4, core: 2. Of those that a mesh axis runs over, the one named last changes fastest.
Arguments:
- queries: bfloat16 [256, 8, 64, 128], P('group', None, 'head'), may hold values from -12 to 12
- fresh_kv: bfloat16 [256, 8, 8, 2, 128], P('group', None, 'head'), may hold values from -4 to 4
- page_pool: bfloat16 [1024, 8, 2, 128, 128], P('group', 'head'), may hold values from -6 to 6
- context_len: int32 [256], P('group'), may hold values from 1 to 1024, as said below
- page_holder: int32 [256, 8], P('group'), may hold values from 0 to 15, as said below
- page_index: int32 [256, 8], P('group'), may hold values from 0 to 63
- hot_owner: int32 [1], replicated, may hold values from 0 to 15
- hot_pages: int32 [32], replicated, may hold values from 0 to 63
Outputs:
- attended: bfloat16 [256, 8, 64, 128], P('group', None, 'head')
Inputs may be any that keep to these rules, and one draw needn't show every extreme that they name: `context_len`: in each decode group of 16 requests one request has exactly 1024 tokens. `page_holder`: among the entries of one decode group's 16 requests each holder group is named at most 8 times; entries of pages past a request's context are not read.
All inputs are finite; a program needn't handle non-finite values.
Results may differ from a plain program's by a relative error of at most 0.02.
Values may be sent and summed in bfloat16 or wider, within the bound.
A program may use at most 192 MiB of HBM per device.

v0:
```python
import math

import jax
import jax.numpy as jnp
from jax import lax
from jax.sharding import PartitionSpec as P

NEG_FILL = -1e30


def spread(value, axis, source):
    kept = jnp.where(lax.axis_index(axis) == source, value, 0).astype(value.dtype)
    return lax.psum(kept, axis)


def hot_partial(query_rows, hot_keys, hot_values, score_scale):
    scores = (
        jnp.einsum("rsxgd,pxtd->rsxgpt", query_rows, hot_keys, preferred_element_type=jnp.float32)
        * score_scale
    )
    row_max = jnp.max(scores, axis=(4, 5))
    exponent = jnp.exp(scores - row_max[:, :, :, :, None, None])
    weight_sum = jnp.sum(exponent, axis=(4, 5))
    weighted = jnp.einsum(
        "rsxgpt,pxtd->rsxgd",
        exponent.astype(jnp.bfloat16),
        hot_values,
        preferred_element_type=jnp.float32,
    )
    return (row_max, weight_sum, weighted)


def page_partial(query_rows, own_pages, usable, score_scale):
    scores = (
        jnp.einsum(
            "rsxgd,rpxtd->rsxgpt",
            query_rows,
            own_pages[:, :, :, 0],
            preferred_element_type=jnp.float32,
        )
        * score_scale
    )
    allowed = usable[:, None, None, None, :, :]
    masked = jnp.where(allowed, scores, NEG_FILL)
    row_max = jnp.max(masked, axis=(4, 5))
    exponent = jnp.where(allowed, jnp.exp(masked - row_max[:, :, :, :, None, None]), 0.0)
    weight_sum = jnp.sum(exponent, axis=(4, 5))
    weighted = jnp.einsum(
        "rsxgpt,rpxtd->rsxgd",
        exponent.astype(jnp.bfloat16),
        own_pages[:, :, :, 1],
        preferred_element_type=jnp.float32,
    )
    return (row_max, weight_sum, weighted)


def fresh_partial(query_rows, fresh_kv, score_scale):
    steps = query_rows.shape[1]
    scores = (
        jnp.einsum(
            "rsxgd,rkxd->rsxgk",
            query_rows,
            fresh_kv[:, :, :, 0],
            preferred_element_type=jnp.float32,
        )
        * score_scale
    )
    step_order = jnp.arange(steps, dtype=jnp.int32)
    allowed = (step_order[None, :] <= step_order[:, None])[None, :, None, None, :]
    masked = jnp.where(allowed, scores, NEG_FILL)
    row_max = jnp.max(masked, axis=4)
    exponent = jnp.where(allowed, jnp.exp(masked - row_max[..., None]), 0.0)
    weight_sum = jnp.sum(exponent, axis=4)
    weighted = jnp.einsum(
        "rsxgk,rkxd->rsxgd",
        exponent.astype(jnp.bfloat16),
        fresh_kv[:, :, :, 1],
        preferred_element_type=jnp.float32,
    )
    return (row_max, weight_sum, weighted)


def combine_partials(row_max, weight_sum, weighted, stack_axis):
    largest = jnp.max(row_max, axis=stack_axis, keepdims=True)
    factor = jnp.exp(row_max - largest)
    total_sum = jnp.sum(weight_sum * factor, axis=stack_axis)
    mixture = jnp.sum(weighted * factor[..., None], axis=stack_axis)
    return (jnp.squeeze(largest, stack_axis), total_sum, mixture)


def on_device(
    queries, fresh_kv, page_pool, context_len, page_holder, page_index, hot_owner, hot_pages
):
    requests, steps, local_heads, head_dim = queries.shape
    kv_local = fresh_kv.shape[2]
    per_kv = local_heads // kv_local
    page_len = page_pool.shape[3]
    max_pages = page_holder.shape[1]
    groups = lax.axis_size("group")
    capacity = max(2, (requests * max_pages + groups - 1) // groups)
    score_scale = 1.0 / math.sqrt(head_dim)
    query_rows = queries.reshape(requests, steps, kv_local, per_kv, head_dim)
    hot_local = jnp.take(page_pool, hot_pages, axis=0)
    hot_kv = spread(hot_local, "group", hot_owner[0])
    hot_keys = hot_kv[:, :, 0]
    hot_values = hot_kv[:, :, 1]
    block_size = math.gcd(requests, max(1, 512 // (steps * per_kv)))
    blocks = requests // block_size

    def hot_block(block_rows):
        return hot_partial(block_rows, hot_keys, hot_values, score_scale)

    def unblock(stacked):
        return stacked.reshape((requests,) + stacked.shape[2:])

    hot_parts = lax.map(
        hot_block, query_rows.reshape(blocks, block_size, steps, kv_local, per_kv, head_dim)
    )
    hot_parts = jax.tree.map(unblock, hot_parts)
    page_order = jnp.arange(max_pages, dtype=jnp.int32)
    token_order = jnp.arange(page_len, dtype=jnp.int32)
    page_count = (context_len + page_len - 1) // page_len
    live_pages = page_order[None, :] < page_count[:, None]
    filled = jnp.clip(context_len[:, None] - page_order[None, :] * page_len, 0, page_len)
    flat_holder = page_holder.reshape(-1)
    flat_live = live_pages.reshape(-1)
    member = (
        (flat_holder[:, None] == jnp.arange(groups, dtype=jnp.int32)[None, :]) & flat_live[:, None]
    ).astype(jnp.int32)
    earlier = jnp.cumsum(member, axis=0) - member
    slot_rank = jnp.sum(earlier * member, axis=1)
    slot_flat = flat_holder * capacity + slot_rank
    gather_slot = jnp.where(flat_live, slot_flat, 0)
    target = jnp.where(flat_live, slot_flat, groups * capacity)
    slot_ids = (
        jnp.zeros((groups * capacity,), jnp.int32)
        .at[target]
        .set(page_index.reshape(-1), mode="drop")
    )
    slot_info = slot_ids.reshape(groups, capacity, 1)
    asked_for = lax.all_to_all(slot_info, "group", split_axis=0, concat_axis=0, tiled=True)
    served = jnp.take(page_pool, asked_for[:, :, 0].reshape(-1), axis=0)
    arrived = lax.all_to_all(
        served.reshape(groups, capacity, kv_local, 2, page_len, head_dim),
        "group",
        split_axis=0,
        concat_axis=0,
        tiled=True,
    )
    own_pages = jnp.take(
        arrived.reshape(groups * capacity, kv_local, 2, page_len, head_dim), gather_slot, axis=0
    )
    own_pages = own_pages.reshape(requests, max_pages, kv_local, 2, page_len, head_dim)
    usable = token_order[None, None, :] < filled[:, :, None]
    private = page_partial(query_rows, own_pages, usable, score_scale)
    fresh_part = fresh_partial(query_rows, fresh_kv, score_scale)
    row_max, weight_sum, weighted = combine_partials(
        jnp.stack((hot_parts[0], private[0], fresh_part[0])),
        jnp.stack((hot_parts[1], private[1], fresh_part[1])),
        jnp.stack((hot_parts[2], private[2], fresh_part[2])),
        0,
    )
    attended = (weighted / weight_sum[..., None]).astype(jnp.bfloat16)
    return attended.reshape(requests, steps, local_heads, head_dim)


def solution(mesh):
    placed = (
        P("group", None, "head", None),
        P("group", None, "head", None, None),
        P("group", "head", None, None, None),
        P("group"),
        P("group", None),
        P("group", None),
        P(),
        P(),
    )
    return jax.shard_map(
        on_device,
        mesh=mesh,
        in_specs=placed,
        out_specs=P("group", None, "head", None),
        check_vma=False,
    )
```

profile of v0, /device:TPU:28, one launch (start us, length us, event | category | flops | bytes accessed | tf_op | source)
XLA Modules:
  0.0 1300.5 jit_solution(16529929433694727963)
XLA Ops:
  10.8 10.0 all_to_all.10
  22.1 18.4 %gather_fusion.1 = bf16[128,4,2,128,128]{4,3,2,1,0:T(8,128)(2,1)} fusion(bf16[64,4,2,128,128]{4,3,2,1,0:T(8,128)(2,1)} %param.12, s32[1024]{0:T(1024)S(1)} %pad_clamp_fusion.1), kind=kCustom, calls=%fused_computation.1 | custom fusion | bytes 67109376 | tf_op jit(solution)/shard_map/jit(_take)/gather | solution.py:142
  40.6 22.9 %copy_select_fusion.1 = bf16[16,8,4,2,128,128]{5,4,1,2,0,3:T(8,128)(2,1)} fusion(bf16[16,8,4,2,128,128]{5,4,3,2,1,0:T(8,128)(2,1)} %bitcast.189, pred[16,8]{1,0:T(8,128)(4,1)S(1)} %compare_and_fusion), kind=kLoop, calls=%fused_computation.21 | loop fusion | flops 16777216 | bytes 67108992 | tf_op jit(solution)/shard_map/jit(_take)/select_n | solution.py:142
  63.5 23.0 %copy.153 = bf16[16,8,4,2,128,128]{5,4,1,2,3,0:T(8,128)(2,1)} copy(bf16[16,8,4,2,128,128]{5,4,1,2,0,3:T(8,128)(2,1)} %copy_select_fusion.1) | data formatting | bytes 67108864 | tf_op jit(solution)/shard_map/jit(_take)/select_n | solution.py:142
  86.5 10.0 all-to-all-start.1
  96.7 10.9 gather_fusion
  108.4 7.6 select_select_fusion
  116.7 6.0 fusion.33
  122.8 3.0 copy.160
  127.8 1.8 copy.164
  131.2 1.8 convolution_bitcast_fusion
  134.4 946.7 %all-reduce.2.cloned.1.call-done = bf16[32,4,2,128,128]{4,3,2,1,0:T(8,128)(2,1)} async-done(((bf16[32,4,2,128,128]{4,3,2,1,0:T(8,128)(2,1)}), bf16[32,4,2,128,128]{4,3,2,1,0:T(8,128)(2,1)}) %all-reduce.2.cloned.1.call-update) | async-done | bytes 8388624 | tf_op jit(solution)/shard_map/psum | solution.py:13
  1081.1 3.8 slice_bitcast_fusion.4
  1084.9 2.3 copy.141
  1087.1 2.4 copy.142
  1089.5 91.0 %while.14 = (s32[]{:T(128)}, f32[2,8,8,4,8]{4,2,3,1,0:T(8,128)S(1)}, f32[2,8,8,4,8]{4,2,3,1,0:T(8,128)}, f32[2,8,8,4,8,128]{5,4,2,3,1,0:T(8,128)}, bf16[2,8,8,4,...) while((s32[]{:T(128)}, ...), condition=%wide.region_4.5_spmd, body=%wide.region_1.4_spmd.sunk | while | flops 4362072064 | bytes 113279080 | solution.py:116
  1089.5 15.5 %bitcast_reduce_fusion.3 = (f32[8,8,4,8]{3,1,0,2:T(8,128)S(1)}, f32[4,8,8,8,32,128]{5,3,4,2,1,0:T(8,128)}) fusion(bf16[32,4,128,128]{3,2,0,1:T(8,128)(2,1)} %get-tuple-element.191, bf16[2,8,8,4,8,128]{5,4,3,2,1,0:T(8,128)(2,1)S(1)} %get-tuple-element.190, s32[]{:T(128)S(6)} %copy.241), kind=kOutput, calls=%fused_computation.5.clone.1 | convolution fusion | flops 2164258816 | bytes 38281220 | tf_op jit(solution)/shard_map/while/body/eval_jaxpr/rsxgd,pxtd->rsxgpt/dot_general | solution.py:18
  1105.0 14.0 %fusion.68 = f32[8,8,4,8]{3,1,0,2:T(8,128)S(1)} fusion(f32[4,8,8,8,32,128]{5,3,4,2,1,0:T(8,128)} %get-tuple-element.167, f32[8,8,4,8]{3,1,0,2:T(8,128)S(1)} %get-tuple-element.166), kind=kLoop, calls=%fused_computation.8.clone.1 | loop fusion | flops 25163776 | bytes 33570816 | tf_op jit(solution)/shard_map/while/body/eval_jaxpr/reduce_sum | solution.py:23
  1119.7 14.3 %fusion.69 = f32[1,8,8,4,8,128]{5,4,2,1,3,0:T(8,128)S(1)} fusion(bf16[32,4,128,128]{3,2,0,1:T(8,128)(2,1)} %get-tuple-element.192, f32[4,8,8,8,32,128]{5,3,4,2,1,0:T(8,128)} %get-tuple-element.167, f32[8,8,4,8]{3,1,0,2:T(8,128)S(1)} %get-tuple-element.166), kind=kOutput, calls=%fused_computation.13.clone.1 | convolution fusion | flops 2172649472 | bytes 38805504 | tf_op jit(solution)/shard_map/while/body/eval_jaxpr/rsxgpt,pxtd->rsxgd/dot_general | solution.py:24
  1134.0 1.1 copy_dynamic-update-slice_fusion.6
  1135.0 15.5 %bitcast_reduce_fusion.3 = (f32[8,8,4,8]{3,1,0,2:T(8,128)S(1)}, f32[4,8,8,8,32,128]{5,3,4,2,1,0:T(8,128)}) fusion(bf16[32,4,128,128]{3,2,0,1:T(8,128)(2,1)} %get-tuple-element.191, bf16[2,8,8,4,8,128]{5,4,3,2,1,0:T(8,128)(2,1)S(1)} %get-tuple-element.190, s32[]{:T(128)S(6)} %copy.241), kind=kOutput, calls=%fused_computation.5.clone.1 | convolution fusion | flops 2164258816 | bytes 38281220 | tf_op jit(solution)/shard_map/while/body/eval_jaxpr/rsxgd,pxtd->rsxgpt/dot_general | solution.py:18
  1150.5 14.0 %fusion.68 = f32[8,8,4,8]{3,1,0,2:T(8,128)S(1)} fusion(f32[4,8,8,8,32,128]{5,3,4,2,1,0:T(8,128)} %get-tuple-element.167, f32[8,8,4,8]{3,1,0,2:T(8,128)S(1)} %get-tuple-element.166), kind=kLoop, calls=%fused_computation.8.clone.1 | loop fusion | flops 25163776 | bytes 33570816 | tf_op jit(solution)/shard_map/while/body/eval_jaxpr/reduce_sum | solution.py:23
  1165.2 14.3 %fusion.69 = f32[1,8,8,4,8,128]{5,4,2,1,3,0:T(8,128)S(1)} fusion(bf16[32,4,128,128]{3,2,0,1:T(8,128)(2,1)} %get-tuple-element.192, f32[4,8,8,8,32,128]{5,3,4,2,1,0:T(8,128)} %get-tuple-element.167, f32[8,8,4,8]{3,1,0,2:T(8,128)S(1)} %get-tuple-element.166), kind=kOutput, calls=%fused_computation.13.clone.1 | convolution fusion | flops 2172649472 | bytes 38805504 | tf_op jit(solution)/shard_map/while/body/eval_jaxpr/rsxgpt,pxtd->rsxgd/dot_general | solution.py:24
  1180.6 23.0 %copy.154 = bf16[16,8,4,2,128,128]{5,4,3,2,1,0:T(8,128)(2,1)} copy(bf16[16,8,4,2,128,128]{5,4,1,2,3,0:T(8,128)(2,1)} %all-to-all-done.1) | data formatting | bytes 67108864 | tf_op jit(solution)/shard_map/all_to_all | solution.py:143
  1203.5 23.9 %gather_fusion.2 = bf16[128,4,2,128,128]{4,3,2,1,0:T(8,128)(2,1)} fusion(bf16[128,4,2,128,128]{4,3,2,1,0:T(8,128)(2,1)} %bitcast.190, s32[1024]{0:T(1024)} %pad_clamp_fusion), kind=kCustom, calls=%fused_computation.2 | custom fusion | bytes 67109376 | tf_op jit(solution)/shard_map/jit(_take)/gather | solution.py:150
  1227.4 22.9 %copy_select_fusion = bf16[16,8,4,2,128,128]{5,4,1,2,0,3:T(8,128)(2,1)} fusion(bf16[16,8,4,2,128,128]{5,4,3,2,1,0:T(8,128)(2,1)} %bitcast.188, pred[16,8]{1,0:T(8,128)(4,1)S(1)} %copy-done.8), kind=kLoop, calls=%fused_computation.20 | loop fusion | flops 16777216 | bytes 67108992 | tf_op jit(solution)/shard_map/jit(_take)/select_n | solution.py:150
  1250.3 12.7 bitcast_reduce_fusion.1
  1263.0 14.7 %fusion.29 = f32[1,16,8,4,8,128]{5,4,2,3,1,0:T(8,128)} fusion(f32[16,4,8,128,8,8]{3,5,4,2,1,0:T(8,128)} %get-tuple-element.118, f32[16,8,4,8]{3,1,2,0:T(8,128)S(1)} %get-tuple-element.117, pred[16,8,128]{2,1,0:T(8,128)(4,1)S(1)} %copy-done.7, bf16[16,8,4,2,128,128]{5,4,1,2,0,3:T(8,128)(2,1)} %copy_select_fusion), kind=kOutput, calls=%fused_computation.47 | convolution fusion | flops 1094713344 | bytes 35946496 | tf_op jit(solution)/shard_map/rsxgpt,rpxtd->rsxgd/dot_general | solution.py:48
  1277.7 8.7 fusion.18
  1286.5 1.2 fusion.37
  1288.1 4.1 fusion.27
  1292.1 1.5 fusion.28
  (71 shorter events, 14.2 us)
Async XLA Ops:
  86.5 10.2 copy-start.10
  86.5 1094.1 %all-to-all-start.1 = ((bf16[16,8,4,2,128,128]{5,4,1,2,3,0:T(8,128)(2,1)}), bf16[16,8,4,2,128,128]{5,4,1,2,3,0:T(8,128)(2,1)}, u32[]{:S(2)}, u32[]{:S(2)}) async-start(bf16[16,8,4,2,128,128]{5,4,1,2,3,0:T(8,128)(2,1)} %copy.153), calls=%async_computation.1 | async-start | bytes 67108864 | tf_op jit(solution)/shard_map/all_to_all | solution.py:143
  96.5 984.6 %all-reduce.2.cloned.1.call-start = ((), (), s32[]{:S(2)}) async-start(), calls=%async_computation.2 | async-start | bytes 16777216 | tf_op jit(solution)/shard_map/psum | solution.py:13
  107.6 8.6 copy-start.3
  107.6 9.1 copy-start
  108.3 24.6 %copy-start.9 = (s32[16]{0:T(128)S(1)}, s32[16]{0:T(128)}, u32[]{:S(2)}) copy-start(s32[16]{0:T(128)} %param.13) | copy-start | bytes 196
  1180.5 105.9 %copy-start.5 = (f32[2,8,8,4,8]{4,2,3,1,0:T(8,128)}, f32[2,8,8,4,8]{4,2,3,1,0:T(8,128)S(1)}, u32[]{:S(2)}) copy-start(f32[2,8,8,4,8]{4,2,3,1,0:T(8,128)S(1)} %get-tuple-element.45) | copy-start | bytes 49156
  1203.5 23.9 %copy-start.8 = (pred[16,8]{1,0:T(8,128)(4,1)S(1)}, pred[16,8]{1,0:T(8,128)(4,1)}, u32[]{:S(2)}) copy-start(pred[16,8]{1,0:T(8,128)(4,1)} %compare_and_fusion.1) | copy-start | bytes 388
  1227.4 22.9 %copy-start.7 = (pred[16,8,128]{2,1,0:T(8,128)(4,1)S(1)}, pred[16,8,128]{2,1,0:T(8,128)(4,1)}, u32[]{:S(2)}) copy-start(pred[16,8,128]{2,1,0:T(8,128)(4,1)} %iota_compare_fusion) | copy-start | bytes 49156
  1277.7 8.7 copy-start.2
  1277.7 8.8 copy-start.4
  1277.7 8.8 copy-start.6
  1277.7 10.3 copy-start.1
Sparse Core Ops, SparseCore 0:
  116.1 964.8 all-reduce.1
where the time goes:
time: 1300 us
  waiting for transfers between devices  947 us (73%)
  local copies, waits for them, and re-layouts  122 us (9%)
  other arithmetic  102 us (8%)
  matrix products  94.7 us (7%)
  between operations  14.4 us (1%)
    psum x1, waiting for transfers between devices, spread(): return lax.psum(kept, axis)  947 us
    dot_general x2, matrix products, hot_partial(): jnp.einsum('rsxgd,pxtd->rsxgpt', query_rows, hot_keys, preferred_element_...  30.9 us
    dot_general x2, matrix products, hot_partial(): jnp.einsum('rsxgpt,pxtd->rsxgd', exponent.astype(jnp.bfloat16), hot_value...  28.5 us
    reduce_sum x2, other arithmetic, hot_partial(): weight_sum = jnp.sum(exponent, axis=(4, 5))  28.1 us
  transfers between devices with their start and end apart: 2, of which 1 were waited for; matrix products, arithmetic and copies ran while one was open for 10% of the time, Pallas kernels for 0%

commit v1 on v0

v1 whole, which is shorter than its diff:
```python
import functools
import math

import jax
import jax.numpy as jnp
from jax import lax
from jax.experimental import pallas as pl
from jax.experimental.pallas import tpu as pltpu
from jax.sharding import PartitionSpec as P

NEG_FILL = -1e30
VMEM_LIMIT = 48 * 1024 * 1024


def spread(value, axis, source):
    kept = jnp.where(lax.axis_index(axis) == source, value, 0).astype(value.dtype)
    return lax.psum(kept, axis)


def rows_by_keys(rows, keys):
    return lax.dot_general(rows, keys, (((1,), (1,)), ((), ())), preferred_element_type=jnp.float32)


def slot_kernel(capacity, kv_local, scale, ids_ref, fill_ref, q_ref, *refs):
    pages, (out_ref, lse_ref) = refs[:capacity], refs[capacity:]
    group = pl.program_id(0)
    rows, page_len = q_ref.shape[3], pages[0].shape[3]
    token = lax.broadcasted_iota(jnp.int32, (rows, page_len), 1)
    lane = lax.broadcasted_iota(jnp.int32, (rows, 128), 1)
    stats = jnp.full((rows, 128), NEG_FILL, jnp.float32)
    for c in range(capacity):
        allowed = token < fill_ref[group * capacity + c]
        for x in range(kv_local):
            scores = rows_by_keys(q_ref[0, c, x], pages[c][0, x, 0]) * scale
            scores = jnp.where(allowed, scores, NEG_FILL)
            top = jnp.max(scores, axis=1, keepdims=True)
            weights = jnp.where(allowed, jnp.exp(scores - top), 0.0)
            total = jnp.maximum(jnp.sum(weights, axis=1, keepdims=True), 1e-30)
            mixed = jnp.dot(
                weights.astype(jnp.bfloat16), pages[c][0, x, 1], preferred_element_type=jnp.float32
            )
            out_ref[0, c, x] = (mixed / total).astype(jnp.bfloat16)
            stats = jnp.where(lane == c * kv_local + x, top + jnp.log(total), stats)
    lse_ref[0] = stats


def slot_attention(slot_pages, slot_fill, slot_queries, page_pool, scale):
    groups, capacity, kv_local, rows, head_dim = slot_queries.shape
    page_len = page_pool.shape[3]

    def page_spec(c):
        return pl.BlockSpec(
            (1, kv_local, 2, page_len, head_dim),
            lambda g, ids, fill: (ids[g * capacity + c], 0, 0, 0, 0),
        )

    block = pl.BlockSpec((1, capacity, kv_local, rows, head_dim), lambda g, ids, fill: (g, 0, 0, 0, 0))
    flops = 4 * groups * capacity * kv_local * rows * page_len * head_dim
    return pl.pallas_call(
        functools.partial(slot_kernel, capacity, kv_local, scale),
        grid_spec=pltpu.PrefetchScalarGridSpec(
            num_scalar_prefetch=2,
            grid=(groups,),
            in_specs=[block] + [page_spec(c) for c in range(capacity)],
            out_specs=[block, pl.BlockSpec((1, rows, 128), lambda g, ids, fill: (g, 0, 0))],
        ),
        out_shape=[
            jax.ShapeDtypeStruct(slot_queries.shape, jnp.bfloat16),
            jax.ShapeDtypeStruct((groups, rows, 128), jnp.float32),
        ],
        compiler_params=pltpu.CompilerParams(vmem_limit_bytes=VMEM_LIMIT),
        cost_estimate=pl.CostEstimate(
            flops=flops, bytes_accessed=64 * 1024 * 1024, transcendentals=flops // (4 * head_dim)
        ),
        name="slot_attention",
    )(slot_pages, slot_fill, slot_queries, page_pool, *([page_pool] * (capacity - 1)))


def hot_kernel(scale, chunk, q_ref, hot_ref, out_ref, lse_ref):
    rows, head_dim = q_ref.shape[1], q_ref.shape[2]
    pages, page_len = hot_ref.shape[0], hot_ref.shape[3]
    q = q_ref[0]

    def step(i, carry):
        top, total, mixed = carry
        keys = hot_ref[pl.ds(i * chunk, chunk), 0, 0].reshape(chunk * page_len, head_dim)
        values = hot_ref[pl.ds(i * chunk, chunk), 0, 1].reshape(chunk * page_len, head_dim)
        scores = rows_by_keys(q, keys) * scale
        new_top = jnp.maximum(top, jnp.max(scores, axis=1, keepdims=True))
        weights = jnp.exp(scores - new_top)
        factor = jnp.exp(top - new_top)
        total = total * factor + jnp.sum(weights, axis=1, keepdims=True)
        mixed = mixed * factor + jnp.dot(
            weights.astype(jnp.bfloat16), values, preferred_element_type=jnp.float32
        )
        return new_top, total, mixed

    top, total, mixed = lax.fori_loop(
        0,
        pages // chunk,
        step,
        (
            jnp.full((rows, 1), NEG_FILL, jnp.float32),
            jnp.zeros((rows, 1), jnp.float32),
            jnp.zeros((rows, head_dim), jnp.float32),
        ),
        unroll=2,
    )
    out_ref[0] = mixed / total
    lse_ref[0] = jnp.broadcast_to(top + jnp.log(total), (rows, 128))


def hot_attention(query_rows, hot_kv, scale):
    kv_local, rows, head_dim = query_rows.shape
    pages, page_len = hot_kv.shape[0], hot_kv.shape[3]
    block = math.gcd(rows, 512)
    flops = 4 * kv_local * rows * pages * page_len * head_dim
    spec = pl.BlockSpec((1, block, head_dim), lambda x, m: (x, m, 0))
    return pl.pallas_call(
        functools.partial(hot_kernel, scale, math.gcd(pages, 4)),
        grid=(kv_local, rows // block),
        in_specs=[spec, pl.BlockSpec((pages, 1, 2, page_len, head_dim), lambda x, m: (0, x, 0, 0, 0))],
        out_specs=[spec, pl.BlockSpec((1, block, 128), lambda x, m: (x, m, 0))],
        out_shape=[
            jax.ShapeDtypeStruct((kv_local, rows, head_dim), jnp.float32),
            jax.ShapeDtypeStruct((kv_local, rows, 128), jnp.float32),
        ],
        compiler_params=pltpu.CompilerParams(vmem_limit_bytes=VMEM_LIMIT),
        cost_estimate=pl.CostEstimate(
            flops=flops, bytes_accessed=16 * 1024 * 1024, transcendentals=flops // (4 * head_dim)
        ),
        name="hot_attention",
    )(query_rows, hot_kv)


def join_kernel(
    max_pages, per_kv, scale, slot_ref, q_ref, fresh_ref, hot_ref, hot_lse_ref, lse_ref, *refs
):
    parts, out_ref = refs[:max_pages], refs[max_pages]
    kv_local, rows, _ = q_ref.shape[1:]
    steps = fresh_ref.shape[3]
    key_step = lax.broadcasted_iota(jnp.int32, (rows, steps), 1)
    row_step = lax.broadcasted_iota(jnp.int32, (rows, steps), 0) // per_kv
    causal = key_step <= row_step
    stats = lse_ref[0]
    for x in range(kv_local):
        fresh = rows_by_keys(q_ref[0, x], fresh_ref[0, x, 0]) * scale
        fresh = jnp.where(causal, fresh, NEG_FILL)
        hot_lse = hot_lse_ref[x][:, :1]
        cols = [stats[:, p * kv_local + x : p * kv_local + x + 1] for p in range(max_pages)]
        top = jnp.maximum(hot_lse, jnp.max(fresh, axis=1, keepdims=True))
        for col in cols:
            top = jnp.maximum(top, col)
        weights = jnp.where(causal, jnp.exp(fresh - top), 0.0)
        hot_weight = jnp.exp(hot_lse - top)
        total = jnp.sum(weights, axis=1, keepdims=True) + hot_weight
        mixed = hot_ref[x] * hot_weight + jnp.dot(
            weights.astype(jnp.bfloat16), fresh_ref[0, x, 1], preferred_element_type=jnp.float32
        )
        for p, col in enumerate(cols):
            share = jnp.exp(col - top)
            total = total + share
            mixed = mixed + parts[p][0, x].astype(jnp.float32) * share
        out_ref[0, x] = (mixed / total).astype(jnp.bfloat16)


def join(slot_of, query_rows, fresh_rows, hot_out, hot_lse, page_lse, parts, per_kv, scale):
    requests, kv_local, rows, head_dim = query_rows.shape
    max_pages = slot_of.shape[0] // requests
    steps = fresh_rows.shape[3]

    def part_spec(p):
        return pl.BlockSpec(
            (1, kv_local, rows, head_dim), lambda r, slot: (slot[r * max_pages + p], 0, 0, 0)
        )

    own = pl.BlockSpec((1, kv_local, rows, head_dim), lambda r, slot: (r, 0, 0, 0))
    return pl.pallas_call(
        functools.partial(join_kernel, max_pages, per_kv, scale),
        grid_spec=pltpu.PrefetchScalarGridSpec(
            num_scalar_prefetch=1,
            grid=(requests,),
            in_specs=[
                own,
                pl.BlockSpec((1, kv_local, 2, steps, head_dim), lambda r, slot: (r, 0, 0, 0, 0)),
                pl.BlockSpec((kv_local, rows, head_dim), lambda r, slot: (0, r, 0)),
                pl.BlockSpec((kv_local, rows, 128), lambda r, slot: (0, r, 0)),
                pl.BlockSpec((1, rows, 128), lambda r, slot: (r, 0, 0)),
            ]
            + [part_spec(p) for p in range(max_pages)],
            out_specs=own,
        ),
        out_shape=jax.ShapeDtypeStruct(query_rows.shape, jnp.bfloat16),
        compiler_params=pltpu.CompilerParams(vmem_limit_bytes=VMEM_LIMIT),
        name="join",
    )(slot_of, query_rows, fresh_rows, hot_out, hot_lse, page_lse, *([parts] * max_pages))


def on_device(
    queries, fresh_kv, page_pool, context_len, page_holder, page_index, hot_owner, hot_pages
):
    requests, steps, local_heads, head_dim = queries.shape
    kv_local = fresh_kv.shape[2]
    per_kv = local_heads // kv_local
    rows = steps * per_kv
    page_len = page_pool.shape[3]
    max_pages = page_holder.shape[1]
    groups = lax.axis_size("group")
    capacity = max(2, (requests * max_pages + groups - 1) // groups)
    slots = groups * capacity
    scale = 1.0 / math.sqrt(head_dim)

    query_rows = queries.reshape(requests, steps, kv_local, per_kv, head_dim)
    query_rows = query_rows.transpose(0, 2, 1, 3, 4).reshape(requests, kv_local, rows, head_dim)
    fresh_rows = fresh_kv.transpose(0, 2, 3, 1, 4)

    page_start = jnp.arange(max_pages, dtype=jnp.int32)[None, :] * page_len
    filled = jnp.clip(context_len[:, None] - page_start, 0, page_len).reshape(-1)
    live = filled > 0
    holder = page_holder.reshape(-1)
    member = (holder[:, None] == jnp.arange(groups, dtype=jnp.int32)[None, :]) & live[:, None]
    member = member.astype(jnp.int32)
    rank = jnp.sum((jnp.cumsum(member, axis=0) - member) * member, axis=1)
    slot_of = jnp.where(live, holder * capacity + rank, slots)
    taken = slot_of[None, :] == jnp.arange(slots, dtype=jnp.int32)[:, None]

    def by_slot(entry):
        return jnp.sum(jnp.where(taken, entry[None, :], 0), axis=1)

    entry_request = jnp.arange(requests * max_pages, dtype=jnp.int32) // max_pages
    slot_request = by_slot(entry_request)
    slot_info = jnp.stack([by_slot(page_index.reshape(-1)), by_slot(filled)], axis=1)
    slot_info = slot_info.reshape(groups, capacity, 2)

    asked = lax.all_to_all(slot_info, "group", split_axis=0, concat_axis=0, tiled=True)
    sent = jnp.take(query_rows, slot_request, axis=0)
    came = lax.all_to_all(
        sent.reshape(groups, capacity, kv_local, rows, head_dim),
        "group",
        split_axis=0,
        concat_axis=0,
        tiled=True,
    )
    hot_local = jnp.take(page_pool, hot_pages, axis=0)
    hot_kv = spread(hot_local, "group", hot_owner[0])
    asked = asked.reshape(slots, 2)
    part, part_lse = slot_attention(asked[:, 0], asked[:, 1], came, page_pool, scale)
    part = lax.all_to_all(part, "group", split_axis=0, concat_axis=0, tiled=True)
    part_lse = lax.all_to_all(part_lse, "group", split_axis=0, concat_axis=0, tiled=True)

    hot_rows = query_rows.transpose(1, 0, 2, 3).reshape(kv_local, requests * rows, head_dim)
    hot_out, hot_lse = hot_attention(hot_rows, hot_kv, scale)

    used = jnp.where(live, slot_of, 0)
    lse = part_lse[:, :, : capacity * kv_local].reshape(groups, rows, capacity, kv_local)
    lse = lse.transpose(0, 2, 1, 3).reshape(slots, rows, kv_local)
    lse = jnp.where(live[:, None, None], jnp.take(lse, used, axis=0), NEG_FILL)
    lse = lse.reshape(requests, max_pages, rows, kv_local).transpose(0, 2, 1, 3)
    lse = lse.reshape(requests, rows, max_pages * kv_local)
    lse = jnp.pad(lse, ((0, 0), (0, 0), (0, 128 - max_pages * kv_local)))
    part = part.reshape(slots, kv_local, rows, head_dim)
    attended = join(used, query_rows, fresh_rows, hot_out, hot_lse, lse, part, per_kv, scale)
    attended = attended.reshape(requests, kv_local, steps, per_kv, head_dim)
    return attended.transpose(0, 2, 1, 3, 4).reshape(requests, steps, local_heads, head_dim)


def solution(mesh):
    placed = (
        P("group", None, "head", None),
        P("group", None, "head", None, None),
        P("group", "head", None, None, None),
        P("group"),
        P("group", None),
        P("group", None),
        P(),
        P(),
    )
    return jax.shard_map(
        on_device,
        mesh=mesh,
        in_specs=placed,
        out_specs=P("group", None, "head", None),
        check_vma=False,
    )
```

time: 1300 us -> 906 us (0.70)
  waiting for transfers between devices: 947 us -> 574 us
  Pallas kernels: 0 us -> 229 us
  matrix products: 94.7 us -> 0 us
  local copies, waits for them, and re-layouts: 122 us -> 28.8 us
  other arithmetic: 102 us -> 16.7 us
    psum x1, waiting for transfers between devices: 947 us -> 385 us  [spread(): return lax.psum(kept, axis)]
    pallas_call x0 -> x3, Pallas kernels: none -> 229 us  [the longest x1 128 us: slot_attention(): pl.pallas_call(functools.partial(slot_kernel, capacity, kv_local, scale),...]
    all_to_all x1 -> x3, waiting for transfers between devices: 0.01 us -> 189 us  [the longest x1 189 us: on_device(): lax.all_to_all(sent.reshape(groups, capacity, kv_local, rows, head_dim),...]
    dot_general x8 -> x0, matrix products: 94.7 us -> none  [the longest x2 30.9 us: hot_partial(): jnp.einsum('rsxgd,pxtd->rsxgpt', query_rows, hot_keys, preferred_element_...]
    reduce_sum x7 -> x2, other arithmetic: 42.9 us -> 0.33 us  [the longest x1 0.18 us: on_device(): rank = jnp.sum((jnp.cumsum(member, axis=0) - member) * member, axis=1)]
    select_n x5, other arithmetic: 46.5 us -> 7.46 us  [the longest x2 7.44 us: on_device(): sent = jnp.take(query_rows, slot_request, axis=0)]
    gather x2, local copies, waits for them, and re-layouts: 42.3 us -> 7.22 us  [the longest x1 6.47 us: on_device(): sent = jnp.take(query_rows, slot_request, axis=0)]
    all_to_all x1 -> x0, local copies, waits for them, and re-layouts: 23 us -> none  [on_device(): lax.all_to_all(served.reshape(groups, capacity, kv_local, 2, page_len, he...]
  transfers between devices with their start and end apart: 2 -> 4, of which waited for: 1 -> 2; matrix products, arithmetic and copies ran while one was open for 10% -> 4% of each run, Pallas kernels for 0% -> 5%
where the time goes in v1:
time: 906 us; the launch traced here: 901 us
  waiting for transfers between devices  574 us (63%)
  Pallas kernels  229 us (25%)
  local copies, waits for them, and re-layouts  28.8 us (3%)
  starting transfers between devices  21.1 us (2%)
  blocking collectives  17.2 us (2%)
  other arithmetic  16.7 us (2%)
  between operations  14.3 us (2%)
    psum x1, waiting for transfers between devices, spread(): return lax.psum(kept, axis)  385 us
    all_to_all x1, waiting for transfers between devices, on_device(): lax.all_to_all(sent.reshape(groups, capacity, kv_local, rows, head_dim),...  189 us
    pallas_call x1, Pallas kernels, slot_attention(): pl.pallas_call(functools.partial(slot_kernel, capacity, kv_local, scale),...  128 us
    pallas_call x1, Pallas kernels, join(): pl.pallas_call(functools.partial(join_kernel, max_pages, per_kv, scale),...  60.3 us
    pallas_call x1, Pallas kernels, hot_attention(): pl.pallas_call(functools.partial(hot_kernel, scale, math.gcd(pages, 4)),...  40.6 us
  transfers between devices with their start and end apart: 4, of which 2 were waited for; matrix products, arithmetic and copies ran while one was open for 4% of the time, Pallas kernels for 5%

profile of v1, /device:TPU:28, one launch (start us, length us, event | category | flops | bytes accessed | tf_op | source)
XLA Modules:
  0.0 901.2 jit_solution(17773380512285675166)
XLA Ops:
  6.5 0.8 subtract_clamp_fusion
  7.4 0.8 copy.54
  8.4 0.2 reduce_window_sum.11
  8.6 0.2 select_reduce_fusion.3
  8.8 0.8 copy.59
  9.6 0.2 select_reduce_fusion
  10.0 0.6 copy.60
  10.6 6.9 all-to-all-start
  17.6 0.5 copy_bitcast_fusion.1
  18.2 6.5 gather_fusion.1
  24.7 7.4 broadcast_select_fusion
  32.1 7.0 all-to-all-start.1
  39.2 188.9 %all-to-all-done.1.q_ref = bf16[16,8,4,64,128]{4,3,2,1,0:T(8,128)(2,1)} async-done(((bf16[16,8,4,64,128]{4,3,2,1,0:T(8,128)(2,1)}), bf16[16,8,4,64,128]{4,3,2,1,0:T(8,128)(2,1)}, u32[]{:S(2)}, u32[]{:S(2)}) %all-to-all-start.1) | async-done | bytes 8388640 | tf_op jit(solution)/shard_map/all_to_all | solution.py:237
  228.1 128.2 %slot_attention.1 = (bf16[16,8,4,64,128]{4,3,2,1,0:T(8,128)(2,1)}, f32[16,64,128]{2,1,0:T(8,128)S(1)}) custom-call(s32[128]{0:T(128)S(1)} %get-tuple-element.23.ids_ref, s32[128]{0:T(128)S(1)} %get-tuple-element.22.fill_ref, bf16[16,8,4,64,128]{4,3,2,1,0:T(8,128)(2,1)} %all-to-all-done.1.q_ref, bf16[64,4,2,128,128]{4,3,2,1,0:T(8,128)(2,1)} %refs_7_.1, ...), custom_call_target="tpu_custom_call" | custom-call | flops 2147483648 | bytes 67108864 | tf_op jit(solution)/shard_map/slot_attention/pallas_call | solution.py:59
  356.3 17.2 %all_to_all.20 = f32[16,64,128]{2,1,0:T(8,128)} all-to-all(f32[16,64,128]{2,1,0:T(8,128)S(1)} %get-tuple-element.11), channel_id=1, replica_groups=mesh['group'=16,'head'=2] {'group'}, dimensions={0} | all-to-all | bytes 1048576 | tf_op jit(solution)/shard_map/all_to_all | solution.py:249
  373.5 7.0 all-to-all-start.3
  380.5 0.2 all-reduce.3.cloned.1.call-start
  380.7 10.8 %gather_fusion = bf16[32,4,2,128,128]{4,3,2,1,0:T(8,128)(2,1)} fusion(bf16[64,4,2,128,128]{4,3,2,1,0:T(8,128)(2,1)} %refs_7_.1, s32[1024]{0:T(1024)S(1)} %pad_clamp_fusion.2), kind=kCustom, calls=%fused_computation | custom fusion | bytes 16777344 | tf_op jit(solution)/shard_map/jit(_take)/gather | solution.py:244
  392.2 7.6 select_select_fusion
  399.9 0.8 copy-done.6
  401.2 385.1 %all-reduce.3.cloned.1.call-done.hot_ref = bf16[32,4,2,128,128]{4,3,2,1,0:T(8,128)(2,1)} async-done(((bf16[32,4,2,128,128]{4,3,2,1,0:T(8,128)(2,1)}), bf16[32,4,2,128,128]{4,3,2,1,0:T(8,128)(2,1)}) %all-reduce.3.cloned.1.call-update) | async-done | bytes 8388624 | tf_op jit(solution)/shard_map/psum | solution.py:17
  786.3 40.6 %hot_attention.1 = (f32[4,1024,128]{2,1,0:T(8,128)S(1)}, f32[4,1024,128]{2,1,0:T(8,128)S(1)}) custom-call(bf16[4,1024,128]{2,1,0:T(8,128)(2,1)S(1)} %bitcast.60, bf16[32,4,2,128,128]{4,3,2,1,0:T(8,128)(2,1)} %all-reduce.3.cloned.1.call-done.hot_ref), custom_call_target="tpu_custom_call" | custom-call | flops 8589934592 | bytes 16777216 | tf_op jit(solution)/shard_map/hot_attention/pallas_call | solution.py:119
  826.9 1.3 copy-done.2
  828.2 1.3 copy-done.4
  829.5 0.2 copy.62
  829.8 0.2 copy.75
  829.9 0.2 copy.64
  830.1 0.7 gather_fusion.2
  831.0 0.2 copy.67
  831.3 1.6 copy-done.3
  832.9 60.3 %join.1 = bf16[16,4,64,128]{3,2,1,0:T(8,128)(2,1)S(1)} custom-call(s32[128]{0:T(128)S(1)} %get-tuple-element.16.slot_ref, bf16[16,4,64,128]{3,2,1,0:T(8,128)(2,1)S(1)} %get-tuple-element.19.q_ref, bf16[16,4,2,8,128]{4,3,2,1,0:T(8,128)(2,1)S(1)} %bitcast.59, f32[4,1024,128]{2,1,0:T(8,128)S(1)} %copy-done.3, f32[4,1024,128]{2,1,0:T(8,128)} %copy-done.4, ...), custom_call_target="tpu_custom_call" | custom-call | tf_op jit(solution)/shard_map/join/pallas_call | solution.py:178
  893.2 1.2 copy_bitcast_fusion
  (50 shorter events, 1.5 us)
Async XLA Ops:
  6.5 11.1 %copy-start = (bf16[16,8,32,128]{3,2,1,0:T(8,128)(2,1)S(1)}, bf16[16,8,32,128]{3,2,1,0:T(8,128)(2,1)}, u32[]{:S(2)}) copy-start(bf16[16,8,32,128]{3,2,1,0:T(8,128)(2,1)} %param.8) | copy-start | bytes 3145732
  10.6 21.5 %all-to-all-start = ((s32[16,8,2]{1,2,0:T(2,128)}), s32[16,8,2]{1,2,0:T(2,128)S(1)}, u32[]{:S(2)}, u32[]{:S(2)}) async-start(s32[16,8,2]{1,2,0:T(2,128)} %copy.60), calls=%async_computation | async-start | bytes 32768 | tf_op jit(solution)/shard_map/all_to_all | solution.py:235
  32.1 196.0 %all-to-all-start.1 = ((bf16[16,8,4,64,128]{4,3,2,1,0:T(8,128)(2,1)}), bf16[16,8,4,64,128]{4,3,2,1,0:T(8,128)(2,1)}, u32[]{:S(2)}, u32[]{:S(2)}) async-start(bf16[16,8,4,64,128]{4,3,2,1,0:T(8,128)(2,1)} %broadcast_select_fusion), calls=%async_computation.1 | async-start | bytes 16777216 | tf_op jit(solution)/shard_map/all_to_all | solution.py:237
  373.5 7.2 copy-start.8
  373.5 457.8 %all-to-all-start.3 = ((bf16[16,8,4,64,128]{4,3,2,1,0:T(8,128)(2,1)}), bf16[16,8,4,64,128]{4,3,2,1,0:T(8,128)(2,1)}, u32[]{:S(2)}, u32[]{:S(2)}) async-start(bf16[16,8,4,64,128]{4,3,2,1,0:T(8,128)(2,1)} %get-tuple-element.12), calls=%async_computation.3 | async-start | bytes 16777216 | tf_op jit(solution)/shard_map/all_to_all | solution.py:248
  380.5 405.8 %all-reduce.3.cloned.1.call-start = ((), (), s32[]{:S(2)}) async-start(), calls=%async_computation.4 | async-start | bytes 16777216 | tf_op jit(solution)/shard_map/psum | solution.py:17
  399.8 0.9 copy-start.6
  399.8 1.1 copy-start.7
  786.3 43.3 %copy-start.5 = (f32[16,64,128]{2,1,0:T(8,128)S(1)}, f32[16,64,128]{2,1,0:T(8,128)}, u32[]{:S(2)}) copy-start(f32[16,64,128]{2,1,0:T(8,128)} %all_to_all.20) | copy-start | bytes 1572868
  826.9 1.3 copy-start.2
  828.2 1.3 copy-start.4
  831.3 1.6 copy-start.3
  832.9 61.5 %copy-start.1 = (bf16[16,8,32,128]{3,2,1,0:T(8,128)(2,1)S(1)}, bf16[16,8,32,128]{3,2,1,0:T(8,128)(2,1)}, u32[]{:S(2)}) copy-start(bf16[16,8,32,128]{3,2,1,0:T(8,128)(2,1)} %param.8) | copy-start | bytes 3145732
Sparse Core Ops, SparseCore 0:
  399.9 386.3 all-reduce.2

commit v2 on v1

--- a/solution.py
+++ b/solution.py
@@ -12,9 +12,8 @@
 VMEM_LIMIT = 48 * 1024 * 1024
 
 
-def spread(value, axis, source):
-    kept = jnp.where(lax.axis_index(axis) == source, value, 0).astype(value.dtype)
-    return lax.psum(kept, axis)
+def kept_by(value, axis, source):
+    return jnp.where(lax.axis_index(axis) == source, value, 0).astype(value.dtype)
 
 
 def rows_by_keys(rows, keys):
@@ -22,26 +21,39 @@
 
 
 def slot_kernel(capacity, kv_local, scale, ids_ref, fill_ref, q_ref, *refs):
-    pages, (out_ref, lse_ref) = refs[:capacity], refs[capacity:]
+    pages, out_ref = refs[:capacity], refs[capacity]
     group = pl.program_id(0)
     rows, page_len = q_ref.shape[3], pages[0].shape[3]
+    batch = math.gcd(capacity, 2)
+    items = batch * kv_local
     token = lax.broadcasted_iota(jnp.int32, (rows, page_len), 1)
     lane = lax.broadcasted_iota(jnp.int32, (rows, 128), 1)
     stats = jnp.full((rows, 128), NEG_FILL, jnp.float32)
-    for c in range(capacity):
-        allowed = token < fill_ref[group * capacity + c]
-        for x in range(kv_local):
-            scores = rows_by_keys(q_ref[0, c, x], pages[c][0, x, 0]) * scale
-            scores = jnp.where(allowed, scores, NEG_FILL)
-            top = jnp.max(scores, axis=1, keepdims=True)
-            weights = jnp.where(allowed, jnp.exp(scores - top), 0.0)
-            total = jnp.maximum(jnp.sum(weights, axis=1, keepdims=True), 1e-30)
-            mixed = jnp.dot(
-                weights.astype(jnp.bfloat16), pages[c][0, x, 1], preferred_element_type=jnp.float32
-            )
-            out_ref[0, c, x] = (mixed / total).astype(jnp.bfloat16)
-            stats = jnp.where(lane == c * kv_local + x, top + jnp.log(total), stats)
-    lse_ref[0] = stats
+    for first in range(0, capacity, batch):
+        pairs = [(c, x) for c in range(first, first + batch) for x in range(kv_local)]
+        scores = []
+        for c, x in pairs:
+            allowed = token < fill_ref[group * capacity + c]
+            score = rows_by_keys(q_ref[0, c, x], pages[c][0, x, 0]) * scale
+            scores.append(jnp.where(allowed, score, NEG_FILL))
+        scores = jnp.stack(scores)
+        top = jnp.max(scores, axis=2, keepdims=True)
+        weights = jnp.where(scores > 0.5 * NEG_FILL, jnp.exp(scores - top), 0.0)
+        total = jnp.maximum(jnp.sum(weights, axis=2, keepdims=True), 1e-30)
+        lse = top + jnp.log(total)
+        inverse = 1.0 / total
+        weights = weights.astype(jnp.bfloat16)
+        for i in range(items):
+            c, x = pairs[i]
+            mixed = jnp.dot(weights[i], pages[c][0, x, 1], preferred_element_type=jnp.float32)
+            out_ref[0, c * kv_local + x] = (mixed * inverse[i]).astype(jnp.bfloat16)
+            stats = jnp.where(lane == c * kv_local + x, lse[i], stats)
+    high = stats.astype(jnp.bfloat16)
+    rest = stats - high.astype(jnp.float32)
+    middle = rest.astype(jnp.bfloat16)
+    low = (rest - middle.astype(jnp.float32)).astype(jnp.bfloat16)
+    for i, term in enumerate((high, middle, low)):
+        out_ref[0, capacity * kv_local + i] = term
 
 
 def slot_attention(slot_pages, slot_fill, slot_queries, page_pool, scale):
@@ -55,6 +67,7 @@
         )
 
     block = pl.BlockSpec((1, capacity, kv_local, rows, head_dim), lambda g, ids, fill: (g, 0, 0, 0, 0))
+    out_rows = capacity * kv_local + 3
     flops = 4 * groups * capacity * kv_local * rows * page_len * head_dim
     return pl.pallas_call(
         functools.partial(slot_kernel, capacity, kv_local, scale),
@@ -62,12 +75,9 @@
             num_scalar_prefetch=2,
             grid=(groups,),
             in_specs=[block] + [page_spec(c) for c in range(capacity)],
-            out_specs=[block, pl.BlockSpec((1, rows, 128), lambda g, ids, fill: (g, 0, 0))],
+            out_specs=pl.BlockSpec((1, out_rows, rows, head_dim), lambda g, ids, fill: (g, 0, 0, 0)),
         ),
-        out_shape=[
-            jax.ShapeDtypeStruct(slot_queries.shape, jnp.bfloat16),
-            jax.ShapeDtypeStruct((groups, rows, 128), jnp.float32),
-        ],
+        out_shape=jax.ShapeDtypeStruct((groups, out_rows, rows, head_dim), jnp.bfloat16),
         compiler_params=pltpu.CompilerParams(vmem_limit_bytes=VMEM_LIMIT),
         cost_estimate=pl.CostEstimate(
             flops=flops, bytes_accessed=64 * 1024 * 1024, transcendentals=flops // (4 * head_dim)
@@ -76,12 +86,12 @@
     )(slot_pages, slot_fill, slot_queries, page_pool, *([page_pool] * (capacity - 1)))
 
 
-def hot_kernel(scale, chunk, q_ref, hot_ref, out_ref, lse_ref):
+def hot_kernel(scale, chunk, q_ref, early_ref, late_ref, out_ref, lse_ref):
     rows, head_dim = q_ref.shape[1], q_ref.shape[2]
-    pages, page_len = hot_ref.shape[0], hot_ref.shape[3]
+    pages, page_len = early_ref.shape[0], early_ref.shape[3]
     q = q_ref[0]
 
-    def step(i, carry):
+    def step(hot_ref, i, carry):
         top, total, mixed = carry
         keys = hot_ref[pl.ds(i * chunk, chunk), 0, 0].reshape(chunk * page_len, head_dim)
         values = hot_ref[pl.ds(i * chunk, chunk), 0, 1].reshape(chunk * page_len, head_dim)
@@ -95,31 +105,31 @@
         )
         return new_top, total, mixed
 
-    top, total, mixed = lax.fori_loop(
-        0,
-        pages // chunk,
-        step,
-        (
-            jnp.full((rows, 1), NEG_FILL, jnp.float32),
-            jnp.zeros((rows, 1), jnp.float32),
-            jnp.zeros((rows, head_dim), jnp.float32),
-        ),
-        unroll=2,
-    )
+    carry = (
+        jnp.full((rows, 1), NEG_FILL, jnp.float32),
+        jnp.zeros((rows, 1), jnp.float32),
+        jnp.zeros((rows, head_dim), jnp.float32),
+    )
+    for hot_ref in (early_ref, late_ref):
+        carry = lax.fori_loop(
+            0, pages // chunk, functools.partial(step, hot_ref), carry, unroll=2
+        )
+    top, total, mixed = carry
     out_ref[0] = mixed / total
     lse_ref[0] = jnp.broadcast_to(top + jnp.log(total), (rows, 128))
 
 
-def hot_attention(query_rows, hot_kv, scale):
+def hot_attention(query_rows, early, late, scale):
     kv_local, rows, head_dim = query_rows.shape
-    pages, page_len = hot_kv.shape[0], hot_kv.shape[3]
+    pages, page_len = early.shape[0], early.shape[3]
     block = math.gcd(rows, 512)
-    flops = 4 * kv_local * rows * pages * page_len * head_dim
+    flops = 8 * kv_local * rows * pages * page_len * head_dim
     spec = pl.BlockSpec((1, block, head_dim), lambda x, m: (x, m, 0))
+    half = pl.BlockSpec((pages, 1, 2, page_len, head_dim), lambda x, m: (0, x, 0, 0, 0))
     return pl.pallas_call(
         functools.partial(hot_kernel, scale, math.gcd(pages, 4)),
         grid=(kv_local, rows // block),
-        in_specs=[spec, pl.BlockSpec((pages, 1, 2, page_len, head_dim), lambda x, m: (0, x, 0, 0, 0))],
+        in_specs=[spec, half, half],
         out_specs=[spec, pl.BlockSpec((1, block, 128), lambda x, m: (x, m, 0))],
         out_shape=[
             jax.ShapeDtypeStruct((kv_local, rows, head_dim), jnp.float32),
@@ -130,7 +140,7 @@
             flops=flops, bytes_accessed=16 * 1024 * 1024, transcendentals=flops // (4 * head_dim)
         ),
         name="hot_attention",
-    )(query_rows, hot_kv)
+    )(query_rows, early, late)
 
 
 def join_kernel(
@@ -147,31 +157,36 @@
         fresh = rows_by_keys(q_ref[0, x], fresh_ref[0, x, 0]) * scale
         fresh = jnp.where(causal, fresh, NEG_FILL)
         hot_lse = hot_lse_ref[x][:, :1]
-        cols = [stats[:, p * kv_local + x : p * kv_local + x + 1] for p in range(max_pages)]
+        page_lse = stats[:, x * max_pages : (x + 1) * max_pages]
         top = jnp.maximum(hot_lse, jnp.max(fresh, axis=1, keepdims=True))
-        for col in cols:
-            top = jnp.maximum(top, col)
+        top = jnp.maximum(top, jnp.max(page_lse, axis=1, keepdims=True))
         weights = jnp.where(causal, jnp.exp(fresh - top), 0.0)
         hot_weight = jnp.exp(hot_lse - top)
+        shares = jnp.exp(page_lse - top)
         total = jnp.sum(weights, axis=1, keepdims=True) + hot_weight
+        total = total + jnp.sum(shares, axis=1, keepdims=True)
         mixed = hot_ref[x] * hot_weight + jnp.dot(
             weights.astype(jnp.bfloat16), fresh_ref[0, x, 1], preferred_element_type=jnp.float32
         )
-        for p, col in enumerate(cols):
-            share = jnp.exp(col - top)
-            total = total + share
-            mixed = mixed + parts[p][0, x].astype(jnp.float32) * share
+        for p in range(max_pages):
+            mixed = mixed + parts[p][0, x].astype(jnp.float32) * shares[:, p : p + 1]
         out_ref[0, x] = (mixed / total).astype(jnp.bfloat16)
 
 
-def join(slot_of, query_rows, fresh_rows, hot_out, hot_lse, page_lse, parts, per_kv, scale):
+def join(capacity, slot_of, query_rows, fresh_rows, hot_out, hot_lse, page_lse, parts, per_kv, scale):
     requests, kv_local, rows, head_dim = query_rows.shape
     max_pages = slot_of.shape[0] // requests
     steps = fresh_rows.shape[3]
 
     def part_spec(p):
         return pl.BlockSpec(
-            (1, kv_local, rows, head_dim), lambda r, slot: (slot[r * max_pages + p], 0, 0, 0)
+            (1, kv_local, rows, head_dim),
+            lambda r, slot: (
+                lax.div(slot[r * max_pages + p], capacity),
+                lax.rem(slot[r * max_pages + p], capacity),
+                0,
+                0,
+            ),
         )
 
     own = pl.BlockSpec((1, kv_local, rows, head_dim), lambda r, slot: (r, 0, 0, 0))
@@ -241,25 +256,31 @@
         concat_axis=0,
         tiled=True,
     )
-    hot_local = jnp.take(page_pool, hot_pages, axis=0)
-    hot_kv = spread(hot_local, "group", hot_owner[0])
+    early, late = jnp.split(hot_pages, 2)
+    early = kept_by(jnp.take(page_pool, early, axis=0), "group", hot_owner[0])
+    late = kept_by(jnp.take(page_pool, late, axis=0), "group", hot_owner[0])
+    early = lax.psum(early, "group")
+    came, early, late = lax.optimization_barrier((came, early, late))
+    late = lax.psum(late, "group")
     asked = asked.reshape(slots, 2)
-    part, part_lse = slot_attention(asked[:, 0], asked[:, 1], came, page_pool, scale)
+    part = slot_attention(asked[:, 0], asked[:, 1], came, page_pool, scale)
+    part, late = lax.optimization_barrier((part, late))
     part = lax.all_to_all(part, "group", split_axis=0, concat_axis=0, tiled=True)
-    part_lse = lax.all_to_all(part_lse, "group", split_axis=0, concat_axis=0, tiled=True)
 
     hot_rows = query_rows.transpose(1, 0, 2, 3).reshape(kv_local, requests * rows, head_dim)
-    hot_out, hot_lse = hot_attention(hot_rows, hot_kv, scale)
+    hot_out, hot_lse = hot_attention(hot_rows, early, late, scale)
 
     used = jnp.where(live, slot_of, 0)
-    lse = part_lse[:, :, : capacity * kv_local].reshape(groups, rows, capacity, kv_local)
+    lse = jnp.sum(part[:, capacity * kv_local :].astype(jnp.float32), axis=1)
+    lse = lse[:, :, : capacity * kv_local].reshape(groups, rows, capacity, kv_local)
     lse = lse.transpose(0, 2, 1, 3).reshape(slots, rows, kv_local)
     lse = jnp.where(live[:, None, None], jnp.take(lse, used, axis=0), NEG_FILL)
-    lse = lse.reshape(requests, max_pages, rows, kv_local).transpose(0, 2, 1, 3)
+    lse = lse.reshape(requests, max_pages, rows, kv_local).transpose(0, 2, 3, 1)
     lse = lse.reshape(requests, rows, max_pages * kv_local)
     lse = jnp.pad(lse, ((0, 0), (0, 0), (0, 128 - max_pages * kv_local)))
-    part = part.reshape(slots, kv_local, rows, head_dim)
-    attended = join(used, query_rows, fresh_rows, hot_out, hot_lse, lse, part, per_kv, scale)
+    attended = join(
+        capacity, used, query_rows, fresh_rows, hot_out, hot_lse, lse, part, per_kv, scale
+    )
     attended = attended.reshape(requests, kv_local, steps, per_kv, head_dim)
     return attended.transpose(0, 2, 1, 3, 4).reshape(requests, steps, local_heads, head_dim)
 

time: 906 us -> 778 us (0.86)
  Pallas kernels: 229 us -> 105 us
    all_to_all x1, waiting for transfers between devices: 189 us -> 0.01 us  [on_device(): lax.all_to_all(sent.reshape(groups, capacity, kv_local, rows, head_dim),...]
    all_to_all x1, waiting for transfers between devices: 0.01 us -> 164 us  [on_device(): lax.all_to_all(part, 'group', split_axis=0, concat_axis=0, tiled=True)]
    pallas_call x1, Pallas kernels: 128 us -> 32.7 us  [slot_attention(): pl.pallas_call(functools.partial(slot_kernel, capacity, kv_local, scale),...]
    psum x1 -> x2, waiting for transfers between devices: 385 us -> 415 us  [the longest x1 284 us: on_device(): early = lax.psum(early, 'group')]
    pallas_call x1, Pallas kernels: 60.3 us -> 31.5 us  [join(): pl.pallas_call(functools.partial(join_kernel, max_pages, per_kv, scale),...]
  transfers between devices with their start and end apart: 4 -> 4, of which waited for: 2 -> 3; matrix products, arithmetic and copies ran while one was open for 4% -> 4% of each run, Pallas kernels for 5% -> 9%
where the time goes in v2:
time: 778 us; the launch traced here: 777 us
  waiting for transfers between devices  579 us (74%)
  Pallas kernels  105 us (13%)
  local copies, waits for them, and re-layouts  34.3 us (4%)
  other arithmetic  20 us (3%)
  between operations  14.3 us (2%)
  starting transfers between devices  14.2 us (2%)
  blocking collectives  10.1 us (1%)
    psum x1, waiting for transfers between devices, on_device(): early = lax.psum(early, 'group')  284 us
    all_to_all x1, waiting for transfers between devices, on_device(): lax.all_to_all(part, 'group', split_axis=0, concat_axis=0, tiled=True)  164 us
    psum x1, waiting for transfers between devices, on_device(): late = lax.psum(late, 'group')  131 us
    pallas_call x1, Pallas kernels, hot_attention(): pl.pallas_call(functools.partial(hot_kernel, scale, math.gcd(pages, 4)),...  41.1 us
    pallas_call x1, Pallas kernels, slot_attention(): pl.pallas_call(functools.partial(slot_kernel, capacity, kv_local, scale),...  32.7 us
    pallas_call x1, Pallas kernels, join(): pl.pallas_call(functools.partial(join_kernel, max_pages, per_kv, scale),...  31.5 us
  transfers between devices with their start and end apart: 4, of which 3 were waited for; matrix products, arithmetic and copies ran while one was open for 4% of the time, Pallas kernels for 9%

profile of v2, /device:TPU:28, one launch (start us, length us, event | category | flops | bytes accessed | tf_op | source)
XLA Modules:
  0.0 777.1 jit_solution(15015550214474617654)
XLA Ops:
  6.5 0.8 subtract_clamp_fusion
  7.5 0.8 copy.52
  8.4 0.2 reduce_window_sum.11
  8.6 0.2 select_reduce_fusion.3
  8.8 0.8 copy.56
  9.6 0.2 select_reduce_fusion.1
  9.9 0.5 copy_bitcast_fusion.1
  10.5 6.5 gather_fusion
  16.9 7.4 broadcast_select_fusion
  24.3 7.1 all-to-all-start
  32.2 8.9 %gather_fusion.2 = bf16[16,4,2,128,128]{4,3,2,1,0:T(8,128)(2,1)} fusion(bf16[64,4,2,128,128]{4,3,2,1,0:T(8,128)(2,1)} %refs_7_.1, s32[1024]{0:T(1024)S(1)} %pad_clamp_fusion.2), kind=kCustom, calls=%fused_computation.clone | custom fusion | bytes 8388672 | tf_op jit(solution)/shard_map/jit(_take)/gather | solution.py:260
  41.1 4.7 select_select_fusion.1
  46.0 8.9 %gather_fusion.3 = bf16[16,4,2,128,128]{4,3,2,1,0:T(8,128)(2,1)} fusion(bf16[64,4,2,128,128]{4,3,2,1,0:T(8,128)(2,1)} %refs_7_.1, s32[1024]{0:T(1024)S(1)} %pad_clamp_fusion.1), kind=kCustom, calls=%fused_computation.1.clone | custom fusion | bytes 8388672 | tf_op jit(solution)/shard_map/jit(_take)/gather | solution.py:261
  54.9 4.8 select_select_fusion
  59.7 284.1 %all-reduce.4.cloned.1.call-done.early_ref = bf16[16,4,2,128,128]{4,3,2,1,0:T(8,128)(2,1)} async-done(((bf16[16,4,2,128,128]{4,3,2,1,0:T(8,128)(2,1)}), bf16[16,4,2,128,128]{4,3,2,1,0:T(8,128)(2,1)}) %all-reduce.4.cloned.1.call-update) | async-done | bytes 4194320 | tf_op jit(solution)/shard_map/psum | solution.py:262
  344.0 10.1 %all_to_all.15 = s32[16,8,2]{1,2,0:T(2,128)S(1)} all-to-all(s32[16,8,2]{1,2,0:T(2,128)S(1)} %copy.57), channel_id=1, replica_groups=mesh['group'=16,'head'=2] {'group'}, dimensions={0} | all-to-all | bytes 2048 | tf_op jit(solution)/shard_map/all_to_all | solution.py:250
  354.2 32.7 %slot_attention.1 = bf16[16,35,64,128]{3,2,1,0:T(8,128)(2,1)} custom-call(s32[128]{0:T(128)S(1)} %get-tuple-element.34.ids_ref, s32[128]{0:T(128)S(1)} %get-tuple-element.33.fill_ref, bf16[16,8,4,64,128]{4,3,2,1,0:T(8,128)(2,1)} %all-to-all-done.q_ref, bf16[64,4,2,128,128]{4,3,2,1,0:T(8,128)(2,1)} %refs_7_.1, bf16[64,4,2,128,128]{4,3,2,1,0:T(8,128)(2,1)} %refs_7_.1, ...), custom_call_target="tpu_custom_call" | custom-call | flops 2147483648 | bytes 67108864 | tf_op jit(solution)/shard_map/slot_attention/pallas_call | solution.py:72
  386.9 130.5 %all-reduce.6.cloned.1.call-done.late_ref = bf16[16,4,2,128,128]{4,3,2,1,0:T(8,128)(2,1)} async-done(((bf16[16,4,2,128,128]{4,3,2,1,0:T(8,128)(2,1)}), bf16[16,4,2,128,128]{4,3,2,1,0:T(8,128)(2,1)}) %all-reduce.6.cloned.1.call-update) | async-done | bytes 4194320 | tf_op jit(solution)/shard_map/psum | solution.py:264
  517.4 7.1 all-to-all-start.2
  525.0 41.1 %hot_attention.1 = (f32[4,1024,128]{2,1,0:T(8,128)S(1)}, f32[4,1024,128]{2,1,0:T(8,128)S(1)}) custom-call(bf16[4,1024,128]{2,1,0:T(8,128)(2,1)S(1)} %bitcast.62, bf16[16,4,2,128,128]{4,3,2,1,0:T(8,128)(2,1)} %all-reduce.4.cloned.1.call-done.early_ref, bf16[16,4,2,128,128]{4,3,2,1,0:T(8,128)(2,1)} %all-reduce.6.cloned.1.call-done.late_ref), custom_call_target="tpu_custom_call" | custom-call | flops 8589934592 | bytes 16777216 | tf_op jit(solution)/shard_map/hot_attention/pallas_call | solution.py:129
  566.1 1.3 copy-done.2
  567.4 1.3 copy-done.4
  568.7 164.2 %all-to-all-done.2.refs_0_.refs_1_.refs_2_.refs_3_.refs_4_.refs_5_.refs_6_.refs_7_ = bf16[16,35,64,128]{3,2,1,0:T(8,128)(2,1)} async-done(((bf16[16,35,64,128]{3,2,1,0:T(8,128)(2,1)}), bf16[16,35,64,128]{3,2,1,0:T(8,128)(2,1)}, u32[]{:S(2)}, u32[]{:S(2)}) %all-to-all-start.2) | async-done | bytes 9175072 | tf_op jit(solution)/shard_map/all_to_all | solution.py:268
  732.9 1.3 convert_reduce_fusion
  734.2 0.2 copy.60
  734.4 0.2 copy.75
  734.6 0.2 copy.62
  734.8 0.8 gather_fusion.1
  735.6 0.2 copy.65
  735.9 1.6 copy-done.3
  737.5 31.5 %join.1 = bf16[16,4,64,128]{3,2,1,0:T(8,128)(2,1)S(1)} custom-call(s32[128]{0:T(128)S(1)} %get-tuple-element.27.slot_ref, bf16[16,4,64,128]{3,2,1,0:T(8,128)(2,1)S(1)} %get-tuple-element.30.q_ref, bf16[16,4,2,8,128]{4,3,2,1,0:T(8,128)(2,1)S(1)} %bitcast.61, f32[4,1024,128]{2,1,0:T(8,128)S(1)} %copy-done.3, f32[4,1024,128]{2,1,0:T(8,128)} %copy-done.4, ...), custom_call_target="tpu_custom_call" | custom-call | tf_op jit(solution)/shard_map/join/pallas_call | solution.py:193
  769.1 1.2 copy_bitcast_fusion
  (50 shorter events, 1.6 us)
Async XLA Ops:
  6.5 3.4 copy-start
  24.3 7.8 %copy-start.6 = (s32[32]{0:T(128)S(1)}, s32[32]{0:T(128)}, u32[]{:S(2)}) copy-start(s32[32]{0:T(128)} %param.17) | copy-start | bytes 388
  24.3 319.4 %all-to-all-start = ((bf16[16,8,4,64,128]{4,3,2,1,0:T(8,128)(2,1)}), bf16[16,8,4,64,128]{4,3,2,1,0:T(8,128)(2,1)}, u32[]{:S(2)}, u32[]{:S(2)}) async-start(bf16[16,8,4,64,128]{4,3,2,1,0:T(8,128)(2,1)} %broadcast_select_fusion), calls=%async_computation | async-start | bytes 16777216 | tf_op jit(solution)/shard_map/all_to_all | solution.py:252
  31.4 312.3 %all-reduce.4.cloned.1.call-start = ((), (), s32[]{:S(2)}) async-start(), calls=%async_computation.3 | async-start | bytes 8388608 | tf_op jit(solution)/shard_map/psum | solution.py:262
  45.9 471.5 %all-reduce.6.cloned.1.call-start = ((), (), s32[]{:S(2)}) async-start(), calls=%async_computation.4 | async-start | bytes 8388608 | tf_op jit(solution)/shard_map/psum | solution.py:264
  386.8 137.8 %copy-start.7 = (s32[16]{0:T(128)S(1)}, s32[16]{0:T(128)}, u32[]{:S(2)}) copy-start(s32[16]{0:T(128)} %param.13) | copy-start | bytes 196
  386.8 138.1 %copy-start.5 = (bf16[16,8,4,2,128]{4,3,2,1,0:T(2,128)(2,1)S(1)}, bf16[16,8,4,2,128]{4,3,2,1,0:T(2,128)(2,1)}, u32[]{:S(2)}) copy-start(bf16[16,8,4,2,128]{4,3,2,1,0:T(2,128)(2,1)} %param.11) | copy-start | bytes 786436
  517.4 215.5 %all-to-all-start.2 = ((bf16[16,35,64,128]{3,2,1,0:T(8,128)(2,1)}), bf16[16,35,64,128]{3,2,1,0:T(8,128)(2,1)}, u32[]{:S(2)}, u32[]{:S(2)}) async-start(bf16[16,35,64,128]{3,2,1,0:T(8,128)(2,1)} %slot_attention.1), calls=%async_computation.2 | async-start | bytes 18350080 | tf_op jit(solution)/shard_map/all_to_all | solution.py:268
  566.1 1.3 copy-start.2
  567.4 1.3 copy-start.4
  735.9 1.6 copy-start.3
  737.5 32.7 %copy-start.1 = (bf16[16,8,32,128]{3,2,1,0:T(8,128)(2,1)S(1)}, bf16[16,8,32,128]{3,2,1,0:T(8,128)(2,1)}, u32[]{:S(2)}) copy-start(bf16[16,8,32,128]{3,2,1,0:T(8,128)(2,1)} %param.10) | copy-start | bytes 3145732
Sparse Core Ops, SparseCore 0:
  46.0 297.6 all-reduce.3
  350.3 167.0 all-reduce.5

commit v3 on v2

--- a/solution.py
+++ b/solution.py
@@ -119,17 +119,19 @@
     lse_ref[0] = jnp.broadcast_to(top + jnp.log(total), (rows, 128))
 
 
-def hot_attention(query_rows, early, late, scale):
+def hot_attention(query_rows, hot_kv, scale):
     kv_local, rows, head_dim = query_rows.shape
-    pages, page_len = early.shape[0], early.shape[3]
+    pages, page_len = hot_kv.shape[0], hot_kv.shape[3]
     block = math.gcd(rows, 512)
-    flops = 8 * kv_local * rows * pages * page_len * head_dim
+    flops = 4 * kv_local * rows * pages * page_len * head_dim
     spec = pl.BlockSpec((1, block, head_dim), lambda x, m: (x, m, 0))
-    half = pl.BlockSpec((pages, 1, 2, page_len, head_dim), lambda x, m: (0, x, 0, 0, 0))
+    half = (pages // 2, 1, 2, page_len, head_dim)
+    early = pl.BlockSpec(half, lambda x, m: (0, x, 0, 0, 0))
+    late = pl.BlockSpec(half, lambda x, m: (1, x, 0, 0, 0))
     return pl.pallas_call(
-        functools.partial(hot_kernel, scale, math.gcd(pages, 4)),
+        functools.partial(hot_kernel, scale, math.gcd(pages // 2, 4)),
         grid=(kv_local, rows // block),
-        in_specs=[spec, half, half],
+        in_specs=[spec, early, late],
         out_specs=[spec, pl.BlockSpec((1, block, 128), lambda x, m: (x, m, 0))],
         out_shape=[
             jax.ShapeDtypeStruct((kv_local, rows, head_dim), jnp.float32),
@@ -140,7 +142,7 @@
             flops=flops, bytes_accessed=16 * 1024 * 1024, transcendentals=flops // (4 * head_dim)
         ),
         name="hot_attention",
-    )(query_rows, early, late)
+    )(query_rows, hot_kv, hot_kv)
 
 
 def join_kernel(
@@ -229,6 +231,12 @@
     query_rows = query_rows.transpose(0, 2, 1, 3, 4).reshape(requests, kv_local, rows, head_dim)
     fresh_rows = fresh_kv.transpose(0, 2, 3, 1, 4)
 
+    hot_kept = kept_by(jnp.take(page_pool, hot_pages, axis=0), "group", hot_owner[0])
+    query_rows, hot_kept = lax.optimization_barrier((query_rows, hot_kept))
+    hot_share = lax.psum_scatter(
+        hot_kept.reshape(-1, head_dim), "group", scatter_dimension=0, tiled=True
+    )
+
     page_start = jnp.arange(max_pages, dtype=jnp.int32)[None, :] * page_len
     filled = jnp.clip(context_len[:, None] - page_start, 0, page_len).reshape(-1)
     live = filled > 0
@@ -256,19 +264,15 @@
         concat_axis=0,
         tiled=True,
     )
-    early, late = jnp.split(hot_pages, 2)
-    early = kept_by(jnp.take(page_pool, early, axis=0), "group", hot_owner[0])
-    late = kept_by(jnp.take(page_pool, late, axis=0), "group", hot_owner[0])
-    early = lax.psum(early, "group")
-    came, early, late = lax.optimization_barrier((came, early, late))
-    late = lax.psum(late, "group")
+    came, hot_share = lax.optimization_barrier((came, hot_share))
+    hot_kv = lax.all_gather(hot_share, "group", axis=0, tiled=True).reshape(hot_kept.shape)
     asked = asked.reshape(slots, 2)
     part = slot_attention(asked[:, 0], asked[:, 1], came, page_pool, scale)
-    part, late = lax.optimization_barrier((part, late))
+    part, hot_kv = lax.optimization_barrier((part, hot_kv))
     part = lax.all_to_all(part, "group", split_axis=0, concat_axis=0, tiled=True)
 
     hot_rows = query_rows.transpose(1, 0, 2, 3).reshape(kv_local, requests * rows, head_dim)
-    hot_out, hot_lse = hot_attention(hot_rows, early, late, scale)
+    hot_out, hot_lse = hot_attention(hot_rows, hot_kv, scale)
 
     used = jnp.where(live, slot_of, 0)
     lse = jnp.sum(part[:, capacity * kv_local :].astype(jnp.float32), axis=1)

time: 778 us -> 677 us (0.87)
  waiting for transfers between devices: 579 us -> 233 us
  blocking collectives: 10.1 us -> 271 us
  local copies, waits for them, and re-layouts: 34.3 us -> 26.4 us
    psum x2 -> x0, waiting for transfers between devices: 415 us -> none  [the longest x1 284 us: on_device(): early = lax.psum(early, 'group')]
    all_to_all x0 -> x1, blocking collectives: none -> 261 us  [on_device(): lax.all_to_all(sent.reshape(groups, capacity, kv_local, rows, head_dim),...]
    all_gather x0 -> x1, waiting for transfers between devices: none -> 69.9 us  [on_device(): lax.all_gather(hot_share, 'group', axis=0, tiled=True)]
    gather x2 -> x1, local copies, waits for them, and re-layouts: 17.8 us -> 10.8 us  [on_device(): jnp.take(page_pool, hot_pages, axis=0)]
  transfers between devices with their start and end apart: 4 -> 3, of which waited for: 3 -> 2; matrix products, arithmetic and copies ran while one was open for 4% -> 2% of each run, Pallas kernels for 9% -> 11%
where the time goes in v3:
time: 677 us; the launch traced here: 676 us
  blocking collectives  271 us (40%)
  waiting for transfers between devices  233 us (34%)
  Pallas kernels  106 us (16%)
  local copies, waits for them, and re-layouts  26.4 us (4%)
  other arithmetic  18.7 us (3%)
  between operations  14.3 us (2%)
  starting transfers between devices  7.17 us (1%)
    all_to_all x1, blocking collectives, on_device(): lax.all_to_all(sent.reshape(groups, capacity, kv_local, rows, head_dim),...  261 us
    all_to_all x1, waiting for transfers between devices, on_device(): lax.all_to_all(part, 'group', split_axis=0, concat_axis=0, tiled=True)  163 us
    all_gather x1, waiting for transfers between devices, on_device(): lax.all_gather(hot_share, 'group', axis=0, tiled=True)  69.9 us
    pallas_call x1, Pallas kernels, hot_attention(): pl.pallas_call(functools.partial(hot_kernel, scale, math.gcd(pages // 2,...  41.1 us
    pallas_call x1, Pallas kernels, slot_attention(): pl.pallas_call(functools.partial(slot_kernel, capacity, kv_local, scale),...  33.4 us
    pallas_call x1, Pallas kernels, join(): pl.pallas_call(functools.partial(join_kernel, max_pages, per_kv, scale),...  31.5 us
  transfers between devices with their start and end apart: 3, of which 2 were waited for; matrix products, arithmetic and copies ran while one was open for 2% of the time, Pallas kernels for 11%

profile of v3, /device:TPU:28, one launch (start us, length us, event | category | flops | bytes accessed | tf_op | source)
XLA Modules:
  0.0 676.1 jit_solution(6629378535727733824)
XLA Ops:
  6.5 0.7 compare_select_fusion.4
  7.3 0.7 compare_and_fusion.2
  8.6 0.3 copy_bitcast_fusion.1.q_ref
  8.9 10.8 %gather_fusion = bf16[32,4,2,128,128]{4,3,2,1,0:T(8,128)(2,1)} fusion(bf16[64,4,2,128,128]{4,3,2,1,0:T(8,128)(2,1)} %refs_7_.1, s32[1024]{0:T(1024)S(1)} %pad_clamp_fusion.2), kind=kCustom, calls=%fused_computation | custom fusion | bytes 16777344 | tf_op jit(solution)/shard_map/jit(_take)/gather | solution.py:234
  19.7 7.6 %select_select_fusion = bf16[32,4,2,128,128]{4,3,2,1,0:T(8,128)(2,1)} fusion(bf16[32,4,2,128,128]{4,3,2,1,0:T(8,128)(2,1)} %gather_fusion, pred[32]{0:T(512)(128)(4,1)S(1)} %compare_and_fusion.2, pred[]{:T(512)S(6)} %eq.32), kind=kLoop, calls=%fused_computation.3 | loop fusion | flops 8388608 | bytes 16777248 | tf_op jit(solution)/shard_map/jit(_where)/select_n | solution.py:16
  27.5 0.6 copy-done.8
  28.4 0.1 fusion.3
  28.5 0.2 reduce_window_sum.11
  28.7 0.2 select_reduce_fusion.3
  29.0 0.2 select_reduce_fusion
  29.3 6.6 gather_fusion.1
  35.9 7.4 %broadcast_select_fusion = bf16[16,8,4,64,128]{4,3,2,1,0:T(8,128)(2,1)} fusion(bf16[16,8,4,64,128]{4,3,2,1,0:T(8,128)(2,1)} %bitcast.64, pred[16,8]{1,0:T(8,128)(4,1)S(1)} %compare_and_fusion.1), kind=kLoop, calls=%fused_computation.4 | loop fusion | flops 4194304 | bytes 16777344 | tf_op jit(solution)/shard_map/jit(_take)/select_n | solution.py:259
  43.3 261.5 %all_to_all.15.q_ref = bf16[16,8,4,64,128]{4,3,2,1,0:T(8,128)(2,1)} all-to-all(bf16[16,8,4,64,128]{4,3,2,1,0:T(8,128)(2,1)} %broadcast_select_fusion), channel_id=1, replica_groups=mesh['group'=16,'head'=2] {'group'}, dimensions={0} | all-to-all | bytes 16777216 | tf_op jit(solution)/shard_map/all_to_all | solution.py:260
  305.0 9.4 %all_to_all.16 = s32[16,8,2]{1,2,0:T(2,128)S(1)} all-to-all(s32[16,8,2]{1,2,0:T(2,128)S(1)} %copy.57), channel_id=1, replica_groups=mesh['group'=16,'head'=2] {'group'}, dimensions={0} | all-to-all | bytes 2048 | tf_op jit(solution)/shard_map/all_to_all | solution.py:258
  314.5 33.4 %slot_attention.1 = bf16[16,35,64,128]{3,2,1,0:T(8,128)(2,1)} custom-call(s32[128]{0:T(128)S(1)} %get-tuple-element.29.ids_ref, s32[128]{0:T(128)S(1)} %get-tuple-element.28.fill_ref, bf16[16,8,4,64,128]{4,3,2,1,0:T(8,128)(2,1)} %all_to_all.15.q_ref, bf16[64,4,2,128,128]{4,3,2,1,0:T(8,128)(2,1)} %refs_7_.1, bf16[64,4,2,128,128]{4,3,2,1,0:T(8,128)(2,1)} %refs_7_.1, ...), custom_call_target="tpu_custom_call" | custom-call | flops 2147483648 | bytes 67108864 | tf_op jit(solution)/shard_map/slot_attention/pallas_call | solution.py:72
  347.9 69.9 %all-gather.2.cloned.1.call-done = bf16[32768,128]{1,0:T(8,128)(2,1)} async-done(((bf16[2048,128]{1,0:T(8,128)(2,1)}), bf16[32768,128]{1,0:T(8,128)(2,1)}) %all-gather.2.cloned.1.call-update) | async-done | bytes 8388624 | tf_op jit(solution)/shard_map/all_gather | solution.py:268
  417.8 7.1 %all-to-all-start.2 = ((bf16[16,35,64,128]{3,2,1,0:T(8,128)(2,1)}), bf16[16,35,64,128]{3,2,1,0:T(8,128)(2,1)}, u32[]{:S(2)}, u32[]{:S(2)}) async-start(bf16[16,35,64,128]{3,2,1,0:T(8,128)(2,1)} %slot_attention.1), calls=%async_computation.3 | async-start | bytes 18350080 | tf_op jit(solution)/shard_map/all_to_all | solution.py:272
  425.0 0.1 copy.55
  425.5 41.1 %hot_attention.1 = (f32[4,1024,128]{2,1,0:T(8,128)S(1)}, f32[4,1024,128]{2,1,0:T(8,128)S(1)}) custom-call(bf16[4,1024,128]{2,1,0:T(8,128)(2,1)S(1)} %bitcast.63, bf16[32,4,2,128,128]{4,3,2,1,0:T(8,128)(2,1)} %bitcast.69, bf16[32,4,2,128,128]{4,3,2,1,0:T(8,128)(2,1)} %bitcast.70), custom_call_target="tpu_custom_call" | custom-call | flops 8589934592 | bytes 16777216 | tf_op jit(solution)/shard_map/hot_attention/pallas_call | solution.py:131
  466.6 1.3 copy-done.2
  468.0 1.3 copy-done.4
  469.3 162.7 %all-to-all-done.2.refs_0_.refs_1_.refs_2_.refs_3_.refs_4_.refs_5_.refs_6_.refs_7_ = bf16[16,35,64,128]{3,2,1,0:T(8,128)(2,1)} async-done(((bf16[16,35,64,128]{3,2,1,0:T(8,128)(2,1)}), bf16[16,35,64,128]{3,2,1,0:T(8,128)(2,1)}, u32[]{:S(2)}, u32[]{:S(2)}) %all-to-all-start.2) | async-done | bytes 9175072 | tf_op jit(solution)/shard_map/all_to_all | solution.py:272
  631.9 1.3 convert_reduce_fusion
  633.3 0.2 copy.60
  633.5 0.2 copy.74
  633.6 0.2 copy.62
  633.8 0.8 gather_fusion.2
  634.6 0.1 copy_bitcast_fusion.2
  634.7 0.2 copy.65
  635.0 1.6 copy-done.3
  636.6 31.5 %join.1 = bf16[16,4,64,128]{3,2,1,0:T(8,128)(2,1)S(1)} custom-call(s32[128]{0:T(128)S(1)} %get-tuple-element.24.slot_ref, bf16[16,4,64,128]{3,2,1,0:T(8,128)(2,1)S(1)} %copy_bitcast_fusion.1.q_ref, bf16[16,4,2,8,128]{4,3,2,1,0:T(8,128)(2,1)S(1)} %bitcast.62, f32[4,1024,128]{2,1,0:T(8,128)S(1)} %copy-done.3, f32[4,1024,128]{2,1,0:T(8,128)} %copy-done.4, ...), custom_call_target="tpu_custom_call" | custom-call | tf_op jit(solution)/shard_map/join/pallas_call | solution.py:195
  668.0 1.2 copy_bitcast_fusion
  (49 shorter events, 1.4 us)
Async XLA Ops:
  6.5 2.1 copy-start
  6.5 298.2 %reduce-scatter.2.cloned.1.call-start = ((), (), s32[]{:S(2)}) async-start(), calls=%async_computation.4 | async-start | bytes 8912896 | tf_op jit(solution)/shard_map/reduce_scatter | solution.py:236
  27.4 0.7 copy-start.8
  27.4 0.8 copy-start.6
  27.4 1.5 copy-start.7
  27.4 390.4 %all-gather.2.cloned.1.call-start = ((), (), s32[]{:S(2)}) async-start(), calls=%async_computation.5 | async-start | bytes 8912896 | tf_op jit(solution)/shard_map/all_gather | solution.py:268
  417.8 7.6 %copy-start.5 = (bf16[16,8,4,2,128]{4,3,2,1,0:T(2,128)(2,1)S(1)}, bf16[16,8,4,2,128]{4,3,2,1,0:T(2,128)(2,1)}, u32[]{:S(2)}) copy-start(bf16[16,8,4,2,128]{4,3,2,1,0:T(2,128)(2,1)} %param.9) | copy-start | bytes 786436
  417.8 214.1 %all-to-all-start.2 = ((bf16[16,35,64,128]{3,2,1,0:T(8,128)(2,1)}), bf16[16,35,64,128]{3,2,1,0:T(8,128)(2,1)}, u32[]{:S(2)}, u32[]{:S(2)}) async-start(bf16[16,35,64,128]{3,2,1,0:T(8,128)(2,1)} %slot_attention.1), calls=%async_computation.3 | async-start | bytes 18350080 | tf_op jit(solution)/shard_map/all_to_all | solution.py:272
  466.6 1.3 copy-start.2
  468.0 1.3 copy-start.4
  635.0 1.6 copy-start.3
  636.5 32.7 %copy-start.1 = (bf16[16,8,32,128]{3,2,1,0:T(8,128)(2,1)S(1)}, bf16[16,8,32,128]{3,2,1,0:T(8,128)(2,1)}, u32[]{:S(2)}) copy-start(bf16[16,8,32,128]{3,2,1,0:T(8,128)(2,1)} %param.8) | copy-start | bytes 3145732
Sparse Core Ops, SparseCore 0:
  27.5 270.3 reduce-scatter.1
  304.9 112.8 all-gather.1
